TPU v7x, 512 devices: a whole 4x4x16 slice. The times are simulated.
512 devices in a mesh: dp: 128 (over z, x, core), grp: 4 (over y).
Axes of the slice: x: 4, y: 4, z: 16, core: 2. Of those that a mesh axis runs over, the one named last changes fastest.
Arguments:
- queries: bfloat16 [32768, 4096], P('dp', 'grp'), may hold values from -6 to 6
- passages: bfloat16 [256, 128, 4096], P(None, 'dp', 'grp'), may hold values from -6 to 6
- block_lists: int32 [256, 3], P('dp'), may hold values from 0 to 255
- list_lengths: int32 [256], P('dp'), may hold values from 1 to 3, as said below
- positive: int32 [32768], P('dp'), may hold values from 0 to 32767, as said below
- loss_grad: float32 [32768], P('dp'), may hold values from -16 to 16
Outputs:
- losses: float32 [32768], P('dp')
- grad_queries: bfloat16 [32768, 4096], P('dp', 'grp')
- grad_passages: bfloat16 [256, 128, 4096], P(None, 'dp', 'grp')
Inputs may be any that keep to these rules, and one draw needn't show every extreme that they name: `block_lists`: entries of a list past its length are ignored. `list_lengths`: the 2 query blocks of one dp index list 4 blocks or fewer together; in every draw some dp index lists exactly 4, with one of its blocks listing 3. positive[q] = n * 128 + r with r == q // 256.
All inputs are finite; a program needn't handle non-finite values.
Results may differ from a plain program's by a relative error of at most 0.0052.
Values may be sent and summed in bfloat16 or wider, within the bound.
A program may use at most 64 MiB of HBM per device.

v0:
```python
import math
import jax
import jax.numpy as jnp
from jax import lax
from jax.sharding import PartitionSpec as P

D = 4096


def pick_rows(selector, table):
    return jnp.sum(jnp.where(selector[:, :, None], table[None], 0.0), axis=1)


def per_device(queries, passages, block_lists, list_lengths, positive, loss_grad):
    score_scale = 3.0 / math.sqrt(D)
    dp_count = lax.axis_size("dp")
    dp_owner = lax.axis_index("dp")
    block_count, list_cap = block_lists.shape
    block_total, shard_rows, feature_width = passages.shape
    block_size = shard_rows * dp_count
    query_rows = queries.shape[0]
    query_blocks = queries.reshape(block_count, block_size, feature_width)
    entry_index = jnp.arange(list_cap, dtype=jnp.int32)
    block_index = jnp.arange(block_count, dtype=jnp.int32)
    slot_count = block_count * list_cap
    slot_block = jnp.repeat(block_index, list_cap)
    slot_ids = block_lists.reshape(slot_count)
    slot_live = (entry_index[None, :] < list_lengths[:, None]).reshape(slot_count)
    all_ids = lax.all_gather(slot_ids, "dp", axis=0, tiled=True)
    outgoing = passages[all_ids].reshape(dp_count, slot_count, shard_rows, feature_width)
    fetched = lax.all_to_all(outgoing, "dp", split_axis=0, concat_axis=2, tiled=True).reshape(
        slot_count, block_size, feature_width
    )
    local_rows = passages.reshape(block_total * shard_rows, feature_width)
    block_match = slot_block[:, None] == block_index[None, :]
    chosen = jnp.einsum(
        "sb,bqf->sqf",
        block_match.astype(jnp.bfloat16),
        query_blocks,
        preferred_element_type=jnp.float32,
    ).astype(jnp.bfloat16)
    part_in = lax.dot_general(
        queries, local_rows, (((1,), (1,)), ((), ())), preferred_element_type=jnp.float32
    )
    part_list = jnp.einsum("sqf,spf->sqp", chosen, fetched, preferred_element_type=jnp.float32)
    full_in, full_list = lax.psum((part_in, part_list), "grp")
    scores_in = score_scale * full_in
    scores_list = score_scale * full_list
    slot_open = block_match & slot_live[:, None]
    slot_peak = jnp.max(scores_list, axis=2)
    list_peak = jnp.max(
        jnp.where(slot_open[:, :, None], slot_peak[:, None, :], -jnp.inf), axis=0
    ).reshape(query_rows)
    row_peak = jnp.maximum(jnp.max(scores_in, axis=1), list_peak)
    slot_shift = pick_rows(block_match, row_peak.reshape(block_count, block_size))
    slot_sums = jnp.sum(jnp.exp(scores_list - slot_shift[:, :, None]), axis=2)
    list_total = jnp.sum(
        jnp.where(slot_open[:, :, None], slot_sums[:, None, :], 0.0), axis=0
    ).reshape(query_rows)
    row_total = jnp.sum(jnp.exp(scores_in - row_peak[:, None]), axis=1) + list_total
    log_total = row_peak + jnp.log(row_total)
    pos_column = positive // block_size * shard_rows + positive % block_size - dp_owner * shard_rows
    column_index = jnp.arange(block_total * shard_rows, dtype=jnp.int32)
    is_positive = column_index[None, :] == pos_column[:, None]
    positive_score = jnp.sum(jnp.where(is_positive, scores_in, 0.0), axis=1)
    losses = log_total - positive_score
    weights_in = (
        loss_grad[:, None]
        * (jnp.exp(scores_in - log_total[:, None]) - is_positive.astype(jnp.float32))
    ).astype(jnp.bfloat16)
    slot_log = pick_rows(block_match, log_total.reshape(block_count, block_size))
    slot_grad = pick_rows(block_match, loss_grad.reshape(block_count, block_size))
    weights_list = jnp.where(
        slot_live[:, None, None],
        slot_grad[:, :, None] * jnp.exp(scores_list - slot_log[:, :, None]),
        0.0,
    ).astype(jnp.bfloat16)
    near_terms = jnp.dot(weights_in, local_rows, preferred_element_type=jnp.float32)
    per_slot = jnp.einsum("sqp,spf->sqf", weights_list, fetched, preferred_element_type=jnp.float32)
    far_terms = jnp.einsum(
        "sb,sqf->bqf", block_match.astype(jnp.float32), per_slot, precision=lax.Precision.HIGHEST
    ).reshape(query_rows, feature_width)
    grad_queries = (score_scale * (near_terms + far_terms)).astype(jnp.bfloat16)
    shares = (
        score_scale
        * jnp.einsum("sqp,sqf->spf", weights_list, chosen, preferred_element_type=jnp.float32)
    ).astype(jnp.bfloat16)
    returned = lax.all_to_all(
        shares.reshape(1, slot_count, block_size, feature_width),
        "dp",
        split_axis=2,
        concat_axis=0,
        tiled=True,
    )
    own_part = score_scale * lax.dot_general(
        weights_in, queries, (((0,), (0,)), ((), ())), preferred_element_type=jnp.float32
    )
    summed = (
        own_part.reshape(block_total, shard_rows, feature_width)
        .at[all_ids]
        .add(returned.reshape(dp_count * slot_count, shard_rows, feature_width).astype(jnp.float32))
    )
    return (losses, grad_queries, summed.astype(jnp.bfloat16))


def solution(mesh):
    in_specs = (P("dp", "grp"), P(None, "dp", "grp"), P("dp", None), P("dp"), P("dp"), P("dp"))
    out_specs = (P("dp"), P("dp", "grp"), P(None, "dp", "grp"))
    return jax.shard_map(
        per_device, mesh=mesh, in_specs=in_specs, out_specs=out_specs, check_vma=False
    )
```

profile of v0, /device:TPU:33, one launch (start us, length us, event | category | flops | bytes accessed | tf_op | source)
XLA Modules:
  0.0 370.0 jit_solution(769956629884457869)
XLA Ops:
  7.2 0.8 reshape.231
  8.0 1.3 dynamic-slice
  9.9 0.2 dynamic-update-slice
  10.2 28.5 %all-reduce = s32[768]{0:T(1024)S(1)} all-reduce(s32[768]{0:T(1024)S(1)} %dynamic-update-slice), channel_id=1, replica_groups=mesh['dp'=128,'grp'=4] {'dp'}, use_global_device_ids=true, to_apply=%add | all-reduce | flops 768 | bytes 6144
  38.7 4.9 %gather_fusion = bf16[768,1024]{1,0:T(8,128)(2,1)S(1)} fusion(bf16[256,1024]{1,0:T(8,128)(2,1)} %bitcast.57, s32[1024]{0:T(1024)S(1)} %pad_clamp_fusion), kind=kCustom, calls=%fused_computation | custom fusion | bytes 3148800 | tf_op jit(solution)/shard_map/gather | solution.py:30
  43.7 1.6 reshape.196
  45.2 14.1 %all-to-all-start = ((bf16[128,6,1,1024]{3,1,2,0:T(8,128)(2,1)}), bf16[128,6,1,1024]{3,1,2,0:T(8,128)(2,1)S(1)}, u32[]{:S(2)}, u32[]{:S(2)}) async-start(bf16[128,6,1,1024]{3,1,2,0:T(8,128)(2,1)} %bitcast.4), calls=%async_computation | async-start | bytes 4194304 | tf_op jit(solution)/shard_map/all_to_all | solution.py:31
  59.5 1.0 fusion.22
  60.6 2.1 fusion.11
  62.7 95.8 %all-to-all-done = bf16[128,6,1,1024]{3,1,2,0:T(8,128)(2,1)S(1)} async-done(((bf16[128,6,1,1024]{3,1,2,0:T(8,128)(2,1)}), bf16[128,6,1,1024]{3,1,2,0:T(8,128)(2,1)S(1)}, u32[]{:S(2)}, u32[]{:S(2)}) %all-to-all-start) | async-done | bytes 1572896 | tf_op jit(solution)/shard_map/all_to_all | solution.py:31
  158.5 4.1 %fusion.4 = f32[6,128,128]{2,1,0:T(8,128)} fusion(bf16[128,6,1,1024]{3,1,2,0:T(8,128)(2,1)S(1)} %all-to-all-done, bf16[6,128,1024]{2,0,1:T(8,128)(2,1)} %fusion.11), kind=kOutput, calls=%fused_computation.9 | convolution fusion | flops 201326592 | bytes 3538944 | tf_op jit(solution)/shard_map/sqf,spf->sqp/dot_general | solution.py:45
  162.8 0.1 copy.53
  163.1 49.7 %all-reduce.4.cloned.1.call-done = (f32[256,256]{1,0:T(8,128)}, f32[6,128,128]{2,1,0:T(8,128)}) async-done(((f32[256,256]{1,0:T(8,128)}, f32[6,128,128]{2,1,0:T(8,128)}), (f32[256,256]{1,0:T(8,128)}, f32[6,128,128]{2,1,0:T(8,128)})) %all-reduce.4.cloned.1.call-update) | async-done | bytes 655376 | tf_op jit(solution)/shard_map/psum | solution.py:46
  212.8 1.1 multiply_reduce_fusion.1
  213.8 1.2 multiply_reduce_fusion
  215.2 1.3 exponential_reduce_fusion
  216.6 1.8 select_reduce_fusion
  218.5 3.9 %fusion.6 = bf16[1,6,128,1024]{3,2,1,0:T(8,128)(2,1)S(1)} fusion(bf16[6,128,1024]{2,0,1:T(8,128)(2,1)} %fusion.11, f32[6,128,128]{2,1,0:T(8,128)} %get-tuple-element.8, f32[6,128]{1,0:T(8,128)S(1)} %get-tuple-element.6, f32[6,128]{1,0:T(8,128)S(1)} %get-tuple-element.5, pred[6]{0:T(512)(128)(4,1)S(1)} %lt.37), kind=kOutput, calls=%fused_computation.11 | convolution fusion | flops 203390976 | bytes 3545094 | tf_op jit(solution)/shard_map/sqp,sqf->spf/dot_general | solution.py:86
  222.5 2.2 copy.57
  224.7 19.1 %all-to-all-start.1 = ((bf16[1,6,128,1024]{3,1,0,2:T(8,128)(2,1)}), bf16[1,6,128,1024]{3,1,0,2:T(8,128)(2,1)}, u32[]{:S(2)}, u32[]{:S(2)}) async-start(bf16[1,6,128,1024]{3,1,0,2:T(8,128)(2,1)} %copy.57), calls=%async_computation.1 | async-start | bytes 4194304 | tf_op jit(solution)/shard_map/all_to_all | solution.py:88
  243.8 2.7 fusion.2
  246.6 3.7 fusion
  250.3 0.3 copy.55
  250.7 0.3 copy-done.7
  251.0 0.6 fusion.24
  251.6 0.5 convolution_multiply_fusion
  252.0 1.2 fusion.8
  253.2 89.4 %all-to-all-done.1 = bf16[1,6,128,1024]{3,1,0,2:T(8,128)(2,1)} async-done(((bf16[1,6,128,1024]{3,1,0,2:T(8,128)(2,1)}), bf16[1,6,128,1024]{3,1,0,2:T(8,128)(2,1)}, u32[]{:S(2)}, u32[]{:S(2)}) %all-to-all-start.1) | async-done | bytes 1572896 | tf_op jit(solution)/shard_map/all_to_all | solution.py:88
  342.6 4.0 %convert_bitcast_fusion = f32[128,1,6,1,1024]{4,2,0,3,1:T(8,128)} fusion(bf16[1,6,128,1024]{3,1,0,2:T(8,128)(2,1)} %all-to-all-done.1), kind=kLoop, calls=%fused_computation.2 | loop fusion | flops 786432 | bytes 4718592 | tf_op jit(solution)/shard_map/convert_element_type | solution.py:101
  346.6 4.8 %reshape.221 = f32[768,1024]{1,0:T(8,128)} reshape(f32[128,1,6,1,1024]{4,2,0,3,1:T(8,128)} %convert_bitcast_fusion) | data formatting | bytes 6291456 | tf_op jit(solution)/shard_map/convert_element_type | solution.py:101
  351.4 10.9 %scatter_fusion = f32[256,1024]{1,0:T(8,128)S(1)} fusion(f32[256,1024]{1,0:T(8,128)S(1)} %convolution_multiply_fusion, s32[768]{0:T(1024)S(1)} %compare_select_fusion, f32[768,1024]{1,0:T(8,128)} %reshape.221), kind=kCustom, calls=%fused_computation.1 | custom fusion | flops 786432 | bytes 9440256 | tf_op jit(solution)/shard_map/scatter-add | solution.py:101
  362.3 0.9 convert_bitcast_fusion.1
  (54 shorter events, 0.9 us)
Async XLA Ops:
  7.2 52.4 %copy-start = (bf16[256,1024]{1,0:T(8,128)(2,1)S(1)}, bf16[256,1024]{1,0:T(8,128)(2,1)}, u32[]{:S(2)}) copy-start(bf16[256,1024]{1,0:T(8,128)(2,1)} %param.6) | copy-start | bytes 1572868
  45.2 14.3 %copy-start.1 = (bf16[256,1,1024]{2,0,1:T(8,128)(2,1)S(1)}, bf16[256,1,1024]{2,0,1:T(8,128)(2,1)}, u32[]{:S(2)}) copy-start(bf16[256,1,1024]{2,0,1:T(8,128)(2,1)} %param.7) | copy-start | bytes 1572868
  45.2 113.3 %all-to-all-start = ((bf16[128,6,1,1024]{3,1,2,0:T(8,128)(2,1)}), bf16[128,6,1,1024]{3,1,2,0:T(8,128)(2,1)S(1)}, u32[]{:S(2)}, u32[]{:S(2)}) async-start(bf16[128,6,1,1024]{3,1,2,0:T(8,128)(2,1)} %bitcast.4), calls=%async_computation | async-start | bytes 4194304 | tf_op jit(solution)/shard_map/all_to_all | solution.py:31
  59.4 153.4 %all-reduce.4.cloned.1.call-start = ((), (), s32[]{:S(2)}) async-start(), calls=%async_computation.2 | async-start | bytes 1310720 | tf_op jit(solution)/shard_map/psum | solution.py:46
  59.5 103.3 %copy-start.12 = (s32[6]{0:T(128)}, s32[6]{0:T(128)S(1)}, u32[]{:S(2)}) copy-start(s32[6]{0:T(128)S(1)} %eq.77) | copy-start | bytes 76
  62.7 100.0 %copy-start.17 = (s32[2]{0:T(128)S(1)}, s32[2]{0:T(128)}, u32[]{:S(2)}) copy-start(s32[2]{0:T(128)} %param.9) | copy-start | bytes 28
  62.7 100.4 %copy-start.16 = (s32[256]{0:T(256)S(1)}, s32[256]{0:T(256)}, u32[]{:S(2)}) copy-start(s32[256]{0:T(256)} %param.10) | copy-start | bytes 3076
  62.7 155.7 %copy-start.4 = (f32[256]{0:T(256)S(1)}, f32[256]{0:T(256)}, u32[]{:S(2)}) copy-start(f32[256]{0:T(256)} %param.11) | copy-start | bytes 3076
  162.8 59.7 %copy-start.14 = (pred[6]{0:T(512)(128)(4,1)}, pred[6]{0:T(512)(128)(4,1)S(1)}, u32[]{:S(2)}) copy-start(pred[6]{0:T(512)(128)(4,1)S(1)} %lt.37) | copy-start | bytes 22
  215.1 7.4 %copy-start.6 = (f32[256]{0:T(256)}, f32[256]{0:T(256)S(1)}, u32[]{:S(2)}) copy-start(f32[256]{0:T(256)S(1)} %bitcast_maximum_fusion.1) | copy-start | bytes 3076
  216.6 1.9 copy-start.10
  218.4 4.1 %copy-start.8 = (f32[256]{0:T(256)}, f32[256]{0:T(256)S(1)}, u32[]{:S(2)}) copy-start(f32[256]{0:T(256)S(1)} %get-tuple-element.4) | copy-start | bytes 3076
  224.7 19.1 %copy-start.2 = (f32[6,128,128]{2,1,0:T(8,128)S(1)}, f32[6,128,128]{2,1,0:T(8,128)}, u32[]{:S(2)}) copy-start(f32[6,128,128]{2,1,0:T(8,128)} %get-tuple-element.8) | copy-start | bytes 1179652
  224.7 117.9 %all-to-all-start.1 = ((bf16[1,6,128,1024]{3,1,0,2:T(8,128)(2,1)}), bf16[1,6,128,1024]{3,1,0,2:T(8,128)(2,1)}, u32[]{:S(2)}, u32[]{:S(2)}) async-start(bf16[1,6,128,1024]{3,1,0,2:T(8,128)(2,1)} %copy.57), calls=%async_computation.1 | async-start | bytes 4194304 | tf_op jit(solution)/shard_map/all_to_all | solution.py:88
  243.8 2.7 copy-start.13
  250.3 0.7 copy-start.7
  250.3 0.7 copy-start.9
  250.3 0.7 copy-start.11
  250.3 0.7 copy-start.15
  250.3 1.2 copy-start.3
  250.3 1.2 copy-start.5
Sparse Core Ops, SparseCore 0:
  162.8 49.9 all-reduce.3
where the time goes:
time: 371 us; the launch traced here: 370 us
  waiting for transfers between devices  235 us (63%)
  starting transfers between devices  33.2 us (9%)
  blocking collectives  28.5 us (8%)
  other arithmetic  22.2 us (6%)
  matrix products  19.2 us (5%)
  local copies, waits for them, and re-layouts  16.9 us (5%)
  between operations  15 us (4%)
    all_to_all x1, waiting for transfers between devices, per_device(): lax.all_to_all(outgoing, 'dp', split_axis=0, concat_axis=2, tiled=True)  95.8 us
    all_to_all x1, waiting for transfers between devices, per_device(): lax.all_to_all(shares.reshape(1, slot_count, block_size, feature_width),...  89.4 us
    psum x1, waiting for transfers between devices, per_device(): full_in, full_list = lax.psum((part_in, part_list), 'grp')  49.7 us
    unnamed x1, blocking collectives  28.5 us
    all_to_all x1, starting transfers between devices, per_device(): lax.all_to_all(shares.reshape(1, slot_count, block_size, feature_width),...  19.1 us
    all_to_all x1, starting transfers between devices, per_device(): lax.all_to_all(outgoing, 'dp', split_axis=0, concat_axis=2, tiled=True)  14.1 us
    scatter-add x1, other arithmetic, per_device(): summed = own_part.reshape(block_total, shard_rows, feature_width).at[all_...  10.9 us
  transfers between devices with their start and end apart: 3, of which 3 were waited for; matrix products, arithmetic and copies ran while one was open for 3% of the time, Pallas kernels for 0%

commit v1 on v0

--- a/solution.py
+++ b/solution.py
@@ -85,12 +85,20 @@
         score_scale
         * jnp.einsum("sqp,sqf->spf", weights_list, chosen, preferred_element_type=jnp.float32)
     ).astype(jnp.bfloat16)
-    returned = lax.all_to_all(
-        shares.reshape(1, slot_count, block_size, feature_width),
-        "dp",
-        split_axis=2,
-        concat_axis=0,
-        tiled=True,
+    returned = jnp.concatenate(
+        lax.all_to_all(
+            jnp.stack(
+                jnp.split(
+                    shares.reshape(1, slot_count, block_size, feature_width),
+                    lax.axis_size("dp"),
+                    axis=2,
+                )
+            ),
+            "dp",
+            0,
+            0,
+        ),
+        axis=0,
     )
     own_part = score_scale * lax.dot_general(
         weights_in, queries, (((0,), (0,)), ((), ())), preferred_element_type=jnp.float32

time: 371 us -> 444 us (1.20)
  local copies, waits for them, and re-layouts: 16.9 us -> 94.1 us
    unnamed x39 -> x166, local copies, waits for them, and re-layouts: 1.89 us -> 78.9 us
where the time goes in v1:
time: 444 us; the launch traced here: 443 us
  waiting for transfers between devices  235 us (53%)
  local copies, waits for them, and re-layouts  94.1 us (21%)
  starting transfers between devices  33.4 us (8%)
  blocking collectives  28.5 us (6%)
  matrix products  19.3 us (4%)
  other arithmetic  17.9 us (4%)
  between operations  15.1 us (3%)
    all_to_all x1, waiting for transfers between devices, per_device(): lax.all_to_all(outgoing, 'dp', split_axis=0, concat_axis=2, tiled=True)  95.6 us
    all_to_all x1, waiting for transfers between devices, per_device(): lax.all_to_all(jnp.stack(jnp.split(shares.reshape(1, slot_count, block_si...  89.4 us
    unnamed x166, local copies, waits for them, and re-layouts  78.9 us
    psum x1, waiting for transfers between devices, per_device(): full_in, full_list = lax.psum((part_in, part_list), 'grp')  49.7 us
    unnamed x1, blocking collectives  28.5 us
    all_to_all x1, starting transfers between devices, per_device(): lax.all_to_all(jnp.stack(jnp.split(shares.reshape(1, slot_count, block_si...  19.1 us
    all_to_all x1, starting transfers between devices, per_device(): lax.all_to_all(outgoing, 'dp', split_axis=0, concat_axis=2, tiled=True)  14.1 us
    scatter-add x1, other arithmetic, per_device(): summed = own_part.reshape(block_total, shard_rows, feature_width).at[all_...  10.7 us
  transfers between devices with their start and end apart: 3, of which 3 were waited for; matrix products, arithmetic and copies ran while one was open for 3% of the time, Pallas kernels for 0%

profile of v1, /device:TPU:33, one launch (start us, length us, event | category | flops | bytes accessed | tf_op | source)
XLA Modules:
  0.0 443.1 jit_solution(2888217242566207737)
XLA Ops:
  7.2 0.8 reshape.226
  8.0 1.3 dynamic-slice
  10.2 28.5 %all-reduce = s32[768]{0:T(1024)S(1)} all-reduce(s32[768]{0:T(1024)S(1)} %dynamic-update-slice), channel_id=1, replica_groups=mesh['dp'=128,'grp'=4] {'dp'}, use_global_device_ids=true, to_apply=%add | all-reduce | flops 768 | bytes 6144
  38.7 4.9 %gather_fusion = bf16[768,1024]{1,0:T(8,128)(2,1)S(1)} fusion(bf16[256,1024]{1,0:T(8,128)(2,1)} %bitcast.308, s32[1024]{0:T(1024)S(1)} %pad_clamp_fusion), kind=kCustom, calls=%fused_computation | custom fusion | bytes 3148800 | tf_op jit(solution)/shard_map/gather | solution.py:30
  43.7 1.6 reshape.192
  45.2 14.1 %all-to-all-start = ((bf16[128,6,1,1024]{3,1,2,0:T(8,128)(2,1)}), bf16[128,6,1,1024]{3,1,2,0:T(8,128)(2,1)S(1)}, u32[]{:S(2)}, u32[]{:S(2)}) async-start(bf16[128,6,1,1024]{3,1,2,0:T(8,128)(2,1)} %bitcast.4), calls=%async_computation | async-start | bytes 4194304 | tf_op jit(solution)/shard_map/all_to_all | solution.py:31
  59.7 1.1 fusion.22
  60.8 2.1 fusion.11
  62.9 95.6 %all-to-all-done = bf16[128,6,1,1024]{3,1,2,0:T(8,128)(2,1)S(1)} async-done(((bf16[128,6,1,1024]{3,1,2,0:T(8,128)(2,1)}), bf16[128,6,1,1024]{3,1,2,0:T(8,128)(2,1)S(1)}, u32[]{:S(2)}, u32[]{:S(2)}) %all-to-all-start) | async-done | bytes 1572896 | tf_op jit(solution)/shard_map/all_to_all | solution.py:31
  158.5 4.1 fusion.4
  163.1 49.7 %all-reduce.4.cloned.1.call-done = (f32[256,256]{1,0:T(8,128)}, f32[6,128,128]{2,1,0:T(8,128)}) async-done(((f32[256,256]{1,0:T(8,128)}, f32[6,128,128]{2,1,0:T(8,128)}), (f32[256,256]{1,0:T(8,128)}, f32[6,128,128]{2,1,0:T(8,128)})) %all-reduce.4.cloned.1.call-update) | async-done | bytes 655376 | tf_op jit(solution)/shard_map/psum | solution.py:46
  212.8 1.1 multiply_reduce_fusion.1
  213.9 1.2 multiply_reduce_fusion
  215.2 1.3 exponential_reduce_fusion
  216.7 1.8 select_reduce_fusion
  218.5 3.9 fusion.6
  231.8 0.6 constant_dynamic-update-slice_fusion.116
  233.6 0.6 constant_dynamic-update-slice_fusion.113
  245.7 0.6 constant_dynamic-update-slice_fusion.93
  262.1 0.6 constant_dynamic-update-slice_fusion.66
  266.4 0.6 constant_dynamic-update-slice_fusion.59
  270.6 0.6 constant_dynamic-update-slice_fusion.52
  272.5 0.6 constant_dynamic-update-slice_fusion.49
  280.3 0.6 constant_dynamic-update-slice_fusion.36
  302.8 19.1 %all-to-all-start.1 = ((bf16[128,1,6,1,1024]{4,2,3,1,0:T(8,128)(2,1)}), bf16[128,1,6,1,1024]{4,2,3,1,0:T(8,128)(2,1)}, u32[]{:S(2)}, u32[]{:S(2)}) async-start(bf16[128,1,6,1,1024]{4,2,3,1,0:T(8,128)(2,1)} %constant_dynamic-update-slice_fusion), calls=%async_computation.1 | async-start | bytes 4194304 | tf_op jit(solution)/shard_map/all_to_all | solution.py:89
  321.9 2.7 fusion.2
  324.6 3.7 fusion
  330.1 1.2 fusion.8
  331.3 89.4 %all-to-all-done.1 = bf16[128,1,6,1,1024]{4,2,3,1,0:T(8,128)(2,1)} async-done(((bf16[128,1,6,1,1024]{4,2,3,1,0:T(8,128)(2,1)}), bf16[128,1,6,1,1024]{4,2,3,1,0:T(8,128)(2,1)}, u32[]{:S(2)}, u32[]{:S(2)}) %all-to-all-start.1) | async-done | bytes 1572896 | tf_op jit(solution)/shard_map/all_to_all | solution.py:89
  420.7 4.0 reshape.216
  424.7 10.7 %scatter_fusion = f32[256,1024]{1,0:T(8,128)S(1)} fusion(f32[256,1024]{1,0:T(8,128)S(1)} %convolution_multiply_fusion, s32[768]{0:T(1024)S(1)} %compare_select_fusion, f32[768,1024]{1,0:T(8,128)} %reshape.216), kind=kCustom, calls=%fused_computation.1 | custom fusion | flops 786432 | bytes 9440256 | tf_op jit(solution)/shard_map/scatter-add | solution.py:109
  435.4 0.9 convert_bitcast_fusion
  (187 shorter events, 78.4 us)
Async XLA Ops:
  7.2 52.5 %copy-start = (bf16[256,1024]{1,0:T(8,128)(2,1)S(1)}, bf16[256,1024]{1,0:T(8,128)(2,1)}, u32[]{:S(2)}) copy-start(bf16[256,1024]{1,0:T(8,128)(2,1)} %param.6) | copy-start | bytes 1572868
  45.2 14.5 %copy-start.1 = (bf16[256,1,1024]{2,0,1:T(8,128)(2,1)S(1)}, bf16[256,1,1024]{2,0,1:T(8,128)(2,1)}, u32[]{:S(2)}) copy-start(bf16[256,1,1024]{2,0,1:T(8,128)(2,1)} %param.7) | copy-start | bytes 1572868
  45.2 113.3 %all-to-all-start = ((bf16[128,6,1,1024]{3,1,2,0:T(8,128)(2,1)}), bf16[128,6,1,1024]{3,1,2,0:T(8,128)(2,1)S(1)}, u32[]{:S(2)}, u32[]{:S(2)}) async-start(bf16[128,6,1,1024]{3,1,2,0:T(8,128)(2,1)} %bitcast.4), calls=%async_computation | async-start | bytes 4194304 | tf_op jit(solution)/shard_map/all_to_all | solution.py:31
  59.4 153.4 %all-reduce.4.cloned.1.call-start = ((), (), s32[]{:S(2)}) async-start(), calls=%async_computation.2 | async-start | bytes 1310720 | tf_op jit(solution)/shard_map/psum | solution.py:46
  59.7 103.1 %copy-start.12 = (s32[6]{0:T(128)}, s32[6]{0:T(128)S(1)}, u32[]{:S(2)}) copy-start(s32[6]{0:T(128)S(1)} %eq.77) | copy-start | bytes 76
  62.9 99.8 %copy-start.17 = (s32[2]{0:T(128)S(1)}, s32[2]{0:T(128)}, u32[]{:S(2)}) copy-start(s32[2]{0:T(128)} %param.9) | copy-start | bytes 28
  62.9 100.2 %copy-start.16 = (s32[256]{0:T(256)S(1)}, s32[256]{0:T(256)}, u32[]{:S(2)}) copy-start(s32[256]{0:T(256)} %param.10) | copy-start | bytes 3076
  62.9 155.6 %copy-start.4 = (f32[256]{0:T(256)S(1)}, f32[256]{0:T(256)}, u32[]{:S(2)}) copy-start(f32[256]{0:T(256)} %param.11) | copy-start | bytes 3076
  162.8 59.7 %copy-start.14 = (pred[6]{0:T(512)(128)(4,1)}, pred[6]{0:T(512)(128)(4,1)S(1)}, u32[]{:S(2)}) copy-start(pred[6]{0:T(512)(128)(4,1)S(1)} %lt.37) | copy-start | bytes 22
  215.1 7.4 %copy-start.6 = (f32[256]{0:T(256)}, f32[256]{0:T(256)S(1)}, u32[]{:S(2)}) copy-start(f32[256]{0:T(256)S(1)} %bitcast_maximum_fusion.1) | copy-start | bytes 3076
  216.6 1.9 copy-start.10
  218.4 4.4 copy-start.8
  302.8 19.1 %copy-start.2 = (f32[6,128,128]{2,1,0:T(8,128)S(1)}, f32[6,128,128]{2,1,0:T(8,128)}, u32[]{:S(2)}) copy-start(f32[6,128,128]{2,1,0:T(8,128)} %get-tuple-element.8) | copy-start | bytes 1179652
  302.8 117.9 %all-to-all-start.1 = ((bf16[128,1,6,1,1024]{4,2,3,1,0:T(8,128)(2,1)}), bf16[128,1,6,1,1024]{4,2,3,1,0:T(8,128)(2,1)}, u32[]{:S(2)}, u32[]{:S(2)}) async-start(bf16[128,1,6,1,1024]{4,2,3,1,0:T(8,128)(2,1)} %constant_dynamic-update-slice_fusion), calls=%async_computation.1 | async-start | bytes 4194304 | tf_op jit(solution)/shard_map/all_to_all | solution.py:89
  321.9 2.7 copy-start.13
  328.3 0.7 copy-start.7
  328.3 0.7 copy-start.9
  328.4 0.7 copy-start.11
  328.4 0.7 copy-start.15
  328.4 1.2 copy-start.3
  328.4 1.2 copy-start.5
Sparse Core Ops, SparseCore 0:
  162.8 49.9 all-reduce.3
